TPU v7x, 128 devices: a whole 4x4x4 slice. The times are simulated.
128 devices in a mesh: face: 16 (over x, z), col: 8 (over y, core).
Axes of the slice: x: 4, y: 4, z: 4, core: 2. Of those that a mesh axis runs over, the one named last changes fastest.
Arguments:
- prognostic: float32 [5, 128, 32, 1024], P(None, None, 'face', 'col'), may hold values from -6 to 6
- diffusivity: float32 [16, 8, 512, 128], P('face', 'col'), may hold values from 0.05 to 5
- surface_flux: float32 [16, 8, 512], P('face', 'col'), may hold values from -8 to 8
- assignment: int32 [16, 8, 256, 1], P('face', 'col'), may hold values from 0 to 127; in each aligned block of 256 rows (0 to 255, 256 to 511, ..., all dimensions but the last counted through in order) at most 4 rows name the same one
Outputs:
- updated: float32 [5, 128, 32, 1024], P(None, None, 'face', 'col')
Inputs may be any that keep to these rules, and one draw needn't show every extreme that they name: `assignment`: among the 256 columns of one device at most 4 have the same owner; some owner gets exactly 4 of them from some device.
All inputs are finite; a program needn't handle non-finite values.
Results may differ from a plain program's by a relative error of at most 0.0003.
Values sent between devices are 32-bit elements; how exact they have to be, the bound alone decides.
A program may use at most 64 MiB of HBM per device.

v0:
```python
import functools

import jax
import jax.numpy as jnp
from jax import lax
from jax.experimental import pallas as pl
from jax.experimental.pallas import tpu as pltpu
from jax.sharding import PartitionSpec as P

MESH = pl.DeviceIdType.MESH
SMOOTHING = 0.2
FACES, COLS = 16, 8
CHIPS = 64
FIELDS, LEVELS, LANES = 5, 128, 128
BLOCKS, STEPS = 8, 16
ROWS = 10
ROOT = FACES - 1
F32, BF16 = jnp.float32, jnp.bfloat16


def split2(value):
    high = value.astype(BF16)
    return high, (value - high.astype(F32)).astype(BF16)


def lookup(table, hot):
    dims = (((0,), (0,)), ((), ()))
    high, low = split2(table)
    return lax.dot_general(high, hot, dims, preferred_element_type=F32) + lax.dot_general(
        low, hot, dims, preferred_element_type=F32
    )


def kernel(
    x_hbm, k_hbm, flux_hbm, assign_hbm, out_hbm,
    xin, target, small, buf, recv, halo, packed, base, work, edge_out, edge_in, hot, kappa_t, out,
    local_sem, swap_send, swap_recv, halo_send, halo_recv, edge_send, edge_recv, all_send, all_recv, out_sem, go_sem,
):
    f, c = lax.axis_index("face"), lax.axis_index("col")
    y, core = c >> 1, c & 1
    chip = f * 4 + y
    up, down = (f + 1) & 15, (f + 15) & 15
    partner = (f, c ^ 1)
    is_root = f == ROOT

    barrier = pltpu.get_barrier_semaphore()
    for r in range(COLS):
        @pl.when(jnp.logical_not(is_root & (c == r)))
        def _():
            pl.semaphore_signal(barrier, inc=1, device_id=(ROOT, r), device_id_type=MESH)
    for peer in ((up, c), (down, c), partner):
        pl.semaphore_signal(barrier, inc=1, device_id=peer, device_id_type=MESH)

    local = [
        pltpu.make_async_copy(x_hbm, xin, local_sem.at[0]),
        pltpu.make_async_copy(assign_hbm, target, local_sem.at[1]),
        pltpu.make_async_copy(k_hbm.at[:, core], buf.at[:, pl.ds(4 * core, 4)], local_sem.at[2]),
        pltpu.make_async_copy(flux_hbm, small.at[core], local_sem.at[3]),
    ]
    for copy in local:
        copy.start()

    @pl.when(is_root)
    def _():
        pl.semaphore_wait(barrier, 3 + FACES * COLS - 1)
        for i in range(FACES - 1):
            pl.semaphore_signal(go_sem, inc=1, device_id=(i, c), device_id_type=MESH)

    @pl.when(jnp.logical_not(is_root))
    def _():
        pl.semaphore_wait(barrier, 3)

    swaps = [
        pltpu.make_async_remote_copy(
            src_ref=src, dst_ref=dst, send_sem=swap_send.at[i], recv_sem=swap_recv.at[i],
            device_id=partner, device_id_type=MESH,
        )
        for i, (src, dst) in enumerate((
            (k_hbm.at[:, 1 - core], buf.at[:, pl.ds(4 * core, 4)]),
            (flux_hbm, small.at[core]),
        ))
    ]
    for copy in swaps:
        copy.start()

    halos = []
    for fl in range(FIELDS):
        at = pl.ds(fl * LEVELS, LEVELS)
        for d, row, peer in ((0, 1, up), (1, 0, down)):
            copy = pltpu.make_async_remote_copy(
                src_ref=x_hbm.at[at, row], dst_ref=halo.at[d, at],
                send_sem=halo_send.at[d, fl], recv_sem=halo_recv.at[d, fl],
                device_id=(peer, c), device_id_type=MESH,
            )
            copy.start()
            halos.append(copy)

    lane = lax.broadcasted_iota(jnp.int32, (8, LANES), 1)
    sub = lax.broadcasted_iota(jnp.int32, (8, LANES), 0)
    local[0].wait()
    x_rows = xin.reshape(FIELDS * LEVELS * 2, LANES)

    def pack(fl, edges):
        edges = list(edges)
        for j in range(STEPS):
            i = fl * STEPS + j
            for r in range(2):
                p = x_rows[pl.ds(fl * 2 * LEVELS + 2 * j + r, BLOCKS, stride=2 * STEPS), :]
                packed[r, fl, j] = p
                edges[r] = jnp.where(lane == i, pltpu.roll(p, i + 1, axis=1), edges[r])
                edges[2 + r] = jnp.where(lane == i, pltpu.roll(p, i, axis=1), edges[2 + r])
        return tuple(edges)

    edges = lax.fori_loop(0, FIELDS, pack, tuple(jnp.zeros((8, LANES), F32) for _ in range(4)))
    for n in range(4):
        edge_out[n // 2, n % 2] = edges[n]

    local[2].wait()
    local[3].wait()
    for copy in swaps:
        copy.wait_recv()
    for s in range(2):
        for g in range(4):
            buf[pl.ds(16 * g, 16), 8 + s] = jnp.broadcast_to(small[s, g], (16, 1, LANES))

    @pl.when(jnp.logical_not(is_root))
    def _():
        pl.semaphore_wait(go_sem, 1)

    for i in range(1, CHIPS):
        pf, py = (f + (i >> 2)) & 15, (y + (i & 3)) & 3
        pltpu.make_async_remote_copy(
            src_ref=buf.at[pf * 4 + py], dst_ref=recv.at[chip], send_sem=all_send, recv_sem=all_recv,
            device_id=(pf, py * 2 + core), device_id_type=MESH,
        ).start()
    own = pltpu.make_async_copy(buf.at[chip], recv.at[chip], local_sem.at[4])
    own.start()
    edge_copies = [
        pltpu.make_async_remote_copy(
            src_ref=edge_out.at[n], dst_ref=edge_in.at[n], send_sem=edge_send.at[n], recv_sem=edge_recv.at[n],
            device_id=(f, (c + step) & 7), device_id_type=MESH,
        )
        for n, step in ((0, 1), (1, 7))
    ]
    for copy in edge_copies:
        copy.start()

    local[1].wait()
    t = target[...]
    owner_hot = (lax.broadcasted_iota(jnp.int32, (FACES * COLS, 256), 0) == t).astype(F32)
    before = (
        lax.broadcasted_iota(jnp.int32, (256, 256), 0) < lax.broadcasted_iota(jnp.int32, (256, 256), 1)
    ).astype(F32)
    running = jnp.dot(owner_hot.astype(BF16), before.astype(BF16), preferred_element_type=F32)
    rank = jnp.sum(owner_hot * running, axis=0, keepdims=True)
    row = ((t >> 1) * ROWS + (t & 1) * 4).astype(F32) + rank
    slots = lax.broadcasted_iota(jnp.int32, (CHIPS * ROWS, 256), 0).astype(F32)
    hot[...] = (slots == row).astype(F32).astype(BF16)

    for copy in edge_copies:
        copy.wait_recv()

    def smooth(fl, carry):
        for j in range(STEPS):
            i = fl * STEPS + j
            for r in range(2):
                p = packed[r, fl, j]
                left = jnp.where(lane == 0, pltpu.roll(edge_in[0, r], LANES - i, axis=1), pltpu.roll(p, 1, axis=1))
                right = jnp.where(
                    lane == LANES - 1,
                    pltpu.roll(edge_in[1, r], LANES - 1 - i, axis=1),
                    pltpu.roll(p, LANES - 1, axis=1),
                )
                base[r, fl, j] = SMOOTHING * (packed[1 - r, fl, j] + left + right - 4.0 * p)
        return carry

    lax.fori_loop(0, FIELDS, smooth, 0)

    own.wait()
    pltpu.make_async_copy(recv.at[pl.ds(0, CHIPS - 1)], recv.at[pl.ds(0, CHIPS - 1)], all_recv).wait()
    received = recv.reshape(CHIPS * ROWS, LANES)
    columns = lookup(received[...], hot[...])
    kappa_t[0] = columns[:, :LANES]
    kappa_t[1] = columns[:, LANES:]
    flux_rows = jnp.concatenate(
        [received[pl.ds(8, CHIPS, stride=ROWS), :], received[pl.ds(9, CHIPS, stride=ROWS), :]], axis=0
    )
    flux_hot = (
        lax.broadcasted_iota(jnp.int32, (FACES * COLS, 256), 0) == (t >> 1) + (t & 1) * CHIPS
    ).astype(F32)
    flux = lookup(flux_rows, flux_hot.astype(BF16))
    wanted = rank + ((f & 3) * 32 + c * 4).astype(F32)
    lanes_at = lax.broadcasted_iota(jnp.int32, (LANES, 256), 0).astype(F32)
    heat = jnp.sum(jnp.where(lanes_at == wanted, flux, 0.0), axis=0, keepdims=True)
    heat = [jnp.where(sub == BLOCKS - 1, heat[:, r * LANES : (r + 1) * LANES], 0.0) for r in range(2)]

    def interface(j):
        return jnp.stack([kappa_t[r, pl.ds(j, BLOCKS, stride=STEPS), :] for r in range(2)])

    subs = jnp.stack([sub, sub])
    ks = [interface(j) for j in range(STEPS)]
    last = jnp.where(subs == BLOCKS - 1, 0.0, ks[-1])
    above = jnp.where(subs == 0, 0.0, pltpu.roll(ks[-1], 1, axis=1))
    q = 1.0 + above
    u = above
    d = packed[:, :, 0]
    work[:, :, 0] = d
    us, rps, gs = [u], [], []
    for j in range(1, STEPS + 1):
        k = ks[j - 1]
        pivot = q + k
        if j == STEPS:
            break
        rp = 1.0 / pivot
        g = k * rp
        q = 1.0 + (k * q) * rp
        d = packed[:, :, j] + g[:, None] * d
        u = g * u
        if j == STEPS - 1:
            d = jnp.concatenate([(d[:, :1] + jnp.stack(heat)[:, None]), d[:, 1:]], axis=1)
        else:
            work[:, :, j] = d
        us.append(u)
        rps.append(rp)
        gs.append(g)
    v = rps[-1][:, None] * work[:, :, STEPS - 2]
    w = gs[-1]
    u0 = rps[-1] * us[STEPS - 2]
    work[:, :, STEPS - 2] = v
    u_all, w_all = [None] * STEPS, [None] * STEPS
    u_all[STEPS - 2], w_all[STEPS - 2] = u0, w
    for j in range(STEPS - 3, -1, -1):
        v = rps[j][:, None] * work[:, :, j] + gs[j][:, None] * v
        u0 = rps[j] * us[j] + gs[j] * u0
        w = gs[j] * w
        work[:, :, j] = v
        u_all[j], w_all[j] = u0, w

    def prev(value, n=1):
        return pltpu.roll(value, n, axis=value.ndim - 2)

    def following(value, n=1):
        return pltpu.roll(value, BLOCKS - n, axis=value.ndim - 2)

    inverse = 1.0 / (pivot - last * following(u0))
    a = us[STEPS - 1] * inverse
    b = last * following(w) * inverse
    rhs = (d + last[:, None] * following(v)) * inverse[:, None]
    for n in (1, 2, 4):
        inverse = 1.0 / (1.0 - a * prev(b, n) - b * following(a, n))
        rhs = (rhs + a[:, None] * prev(rhs, n) + b[:, None] * following(rhs, n)) * inverse[:, None]
        a, b = a * prev(a, n) * inverse, b * following(b, n) * inverse
    bottom = rhs
    top = jnp.where(subs[:, None] == 0, 0.0, prev(bottom))
    for j in range(STEPS - 1):
        base[:, :, j] += work[:, :, j] + u_all[j][:, None] * top + w_all[j][:, None] * bottom
    base[:, :, STEPS - 1] += bottom

    halo_rows = halo.reshape(2 * FIELDS * LEVELS, LANES)
    out_rows = out.reshape(FIELDS * LEVELS * 2, LANES)
    outs = []
    for fl in range(FIELDS):
        for d_at in range(2):
            halos[2 * fl + d_at].wait_recv()
        for j in range(STEPS):
            for r in range(2):
                beside = halo_rows[pl.ds((r * FIELDS + fl) * LEVELS + j, BLOCKS, stride=STEPS), :]
                out_rows[pl.ds(fl * 2 * LEVELS + 2 * j + r, BLOCKS, stride=2 * STEPS), :] = (
                    base[r, fl, j] + SMOOTHING * beside
                )
        at = pl.ds(fl * LEVELS, LEVELS)
        copy = pltpu.make_async_copy(out.at[at], out_hbm.at[at], out_sem.at[fl])
        copy.start()
        outs.append(copy)

    pltpu.make_async_copy(recv.at[pl.ds(0, CHIPS - 1)], recv.at[pl.ds(0, CHIPS - 1)], all_send).wait()
    for copy in swaps + edge_copies + halos:
        copy.wait_send()
    for copy in outs:
        copy.wait()


def shards(prognostic, diffusivity, surface_flux, assignment):
    x = prognostic.reshape(FIELDS * LEVELS, 2, 1, LANES)
    k = diffusivity.reshape(CHIPS, 2, 4, 1, LEVELS)
    flux = surface_flux.reshape(4, 1, LANES)
    target = assignment.reshape(1, 256)
    any_spec = pl.BlockSpec(memory_space=pl.ANY)
    dma = pltpu.SemaphoreType.DMA
    wide = (2, FIELDS, STEPS, BLOCKS, LANES)
    result = pl.pallas_call(
        kernel,
        out_shape=jax.ShapeDtypeStruct(x.shape, F32),
        in_specs=[any_spec] * 4,
        out_specs=any_spec,
        scratch_shapes=[
            pltpu.VMEM(x.shape, F32),
            pltpu.VMEM((1, 256), jnp.int32),
            pltpu.VMEM((2, 4, 1, LANES), F32),
            pltpu.VMEM((CHIPS, ROWS, 1, LANES), F32),
            pltpu.VMEM((CHIPS, ROWS, 1, LANES), F32),
            pltpu.VMEM((2, FIELDS * LEVELS, 1, LANES), F32),
            pltpu.VMEM(wide, F32),
            pltpu.VMEM(wide, F32),
            pltpu.VMEM(wide, F32),
            pltpu.VMEM((2, 2, BLOCKS, LANES), F32),
            pltpu.VMEM((2, 2, BLOCKS, LANES), F32),
            pltpu.VMEM((CHIPS * ROWS, 256), BF16),
            pltpu.VMEM((2, LEVELS, LANES), F32),
            pltpu.VMEM(x.shape, F32),
            dma((5,)),
            dma((2,)),
            dma((2,)),
            dma((2, FIELDS)),
            dma((2, FIELDS)),
            dma((2,)),
            dma((2,)),
            dma,
            dma,
            dma((FIELDS,)),
            pltpu.SemaphoreType.REGULAR,
        ],
        compiler_params=pltpu.CompilerParams(
            collective_id=0, has_side_effects=True, vmem_limit_bytes=56 << 20
        ),
    )(x, k, flux, target)
    return result.reshape(prognostic.shape)


def solution(mesh):
    return jax.shard_map(
        shards,
        mesh=mesh,
        in_specs=(
            P(None, None, "face", "col"),
            P("face", "col", None, None),
            P("face", "col", None),
            P("face", "col", None, None),
        ),
        out_specs=P(None, None, "face", "col"),
        check_vma=False,
    )
```

profile of v0, /device:TPU:0, one launch (start us, length us, event | category | flops | bytes accessed | tf_op | source)
XLA Modules:
  0.0 28.6 jit_solution(8708699705673778326)
XLA Ops:
  0.0 26.6 %shard_map.46 = f32[640,2,1,128]{3,2,1,0:T(1,128)} custom-call(f32[640,2,1,128]{3,2,1,0:T(1,128)} %bitcast.6, f32[64,2,4,1,128]{4,3,2,1,0:T(1,128)} %bitcast.7, f32[4,1,128]{2,1,0:T(1,128)} %bitcast.8, s32[1,256]{1,0:T(1,128)} %bitcast.9), custom_call_target="tpu_custom_call" | custom-call | tf_op jit(solution)/shard_map/pallas_call | solution.py:291
  26.6 2.0 %copy.6 = f32[5,128,2,128]{3,2,1,0:T(2,128)} copy(f32[5,128,2,128]{3,2,1,0:T(2,128)} %bitcast.5) | data formatting | bytes 1310720
where the time goes:
time: 28.7 us; the launch traced here: 28.6 us
  Pallas kernels  26.6 us (93%)
  local copies, waits for them, and re-layouts  1.97 us (7%)
    pallas_call x1, Pallas kernels, shards(): pl.pallas_call(kernel, out_shape=jax.ShapeDtypeStruct(x.shape, F32), in_s...  26.6 us
    unnamed x1, local copies, waits for them, and re-layouts  1.97 us

commit v1 on v0

--- a/solution.py
+++ b/solution.py
@@ -14,7 +14,7 @@
 FIELDS, LEVELS, LANES = 5, 128, 128
 BLOCKS, STEPS = 8, 16
 ROWS = 10
-ROOT = FACES - 1
+ROOT = 13
 F32, BF16 = jnp.float32, jnp.bfloat16
 
 
@@ -32,9 +32,9 @@
 
 
 def kernel(
-    x_hbm, k_hbm, flux_hbm, assign_hbm, out_hbm,
-    xin, target, small, buf, recv, halo, packed, base, work, edge_out, edge_in, hot, kappa_t, out,
-    local_sem, swap_send, swap_recv, halo_send, halo_recv, edge_send, edge_recv, all_send, all_recv, out_sem, go_sem,
+    x_hbm, k_hbm, flux_hbm, assign_hbm, out,
+    xin, target, small, buf, recv, halo, packed, base, work, edge_out, edge_in, hot, kappa_t,
+    local_sem, swap_send, swap_recv, halo_send, halo_recv, edge_send, edge_recv, all_send, all_recv, go_sem,
 ):
     f, c = lax.axis_index("face"), lax.axis_index("col")
     y, core = c >> 1, c & 1
@@ -63,7 +63,7 @@
     @pl.when(is_root)
     def _():
         pl.semaphore_wait(barrier, 3 + FACES * COLS - 1)
-        for i in range(FACES - 1):
+        for i in [j for j in range(FACES) if j != ROOT]:
             pl.semaphore_signal(go_sem, inc=1, device_id=(i, c), device_id_type=MESH)
 
     @pl.when(jnp.logical_not(is_root))
@@ -268,11 +268,6 @@
                 out_rows[pl.ds(fl * 2 * LEVELS + 2 * j + r, BLOCKS, stride=2 * STEPS), :] = (
                     base[r, fl, j] + SMOOTHING * beside
                 )
-        at = pl.ds(fl * LEVELS, LEVELS)
-        copy = pltpu.make_async_copy(out.at[at], out_hbm.at[at], out_sem.at[fl])
-        copy.start()
-        outs.append(copy)
-
     pltpu.make_async_copy(recv.at[pl.ds(0, CHIPS - 1)], recv.at[pl.ds(0, CHIPS - 1)], all_send).wait()
     for copy in swaps + edge_copies + halos:
         copy.wait_send()
@@ -290,9 +285,10 @@
     wide = (2, FIELDS, STEPS, BLOCKS, LANES)
     result = pl.pallas_call(
         kernel,
-        out_shape=jax.ShapeDtypeStruct(x.shape, F32),
+        out_shape=pltpu.VMEM(x.shape, F32),
+        name="exchange",
         in_specs=[any_spec] * 4,
-        out_specs=any_spec,
+        out_specs=pl.BlockSpec(memory_space=pltpu.VMEM),
         scratch_shapes=[
             pltpu.VMEM(x.shape, F32),
             pltpu.VMEM((1, 256), jnp.int32),
@@ -307,7 +303,6 @@
             pltpu.VMEM((2, 2, BLOCKS, LANES), F32),
             pltpu.VMEM((CHIPS * ROWS, 256), BF16),
             pltpu.VMEM((2, LEVELS, LANES), F32),
-            pltpu.VMEM(x.shape, F32),
             dma((5,)),
             dma((2,)),
             dma((2,)),
@@ -317,7 +312,6 @@
             dma((2,)),
             dma,
             dma,
-            dma((FIELDS,)),
             pltpu.SemaphoreType.REGULAR,
         ],
         compiler_params=pltpu.CompilerParams(

time: 28.7 us -> 23.9 us (0.83)
  the two profiles are of different devices: /device:TPU:0 before, /device:TPU:1 now
where the time goes in v1:
time: 23.9 us; the launch traced here: 23.5 us
  Pallas kernels  22.7 us (95%)
  local copies, waits for them, and re-layouts  0.84 us (4%)
    pallas_call x1, Pallas kernels, shards(): pl.pallas_call(kernel, out_shape=pltpu.VMEM(x.shape, F32), name='exchange...  22.7 us
    unnamed x1, local copies, waits for them, and re-layouts  0.84 us

profile of v1, /device:TPU:1, one launch (start us, length us, event | category | flops | bytes accessed | tf_op | source)
XLA Modules:
  0.0 23.5 jit_solution(727290060065660067)
XLA Ops:
  0.0 22.7 %exchange.1 = f32[640,2,1,128]{3,2,1,0:T(1,128)S(1)} custom-call(f32[640,2,1,128]{3,2,1,0:T(1,128)} %bitcast.6, f32[64,2,4,1,128]{4,3,2,1,0:T(1,128)} %bitcast.7, f32[4,1,128]{2,1,0:T(1,128)} %bitcast.8, s32[1,256]{1,0:T(1,128)} %bitcast.9), custom_call_target="tpu_custom_call" | custom-call | tf_op jit(solution)/shard_map/exchange/pallas_call | solution.py:286
  22.7 0.8 %copy.6 = f32[5,128,2,128]{3,2,1,0:T(2,128)} copy(f32[5,128,2,128]{3,2,1,0:T(2,128)S(1)} %bitcast.5) | data formatting | bytes 1310720

commit v2 on v1

--- a/solution.py
+++ b/solution.py
@@ -13,8 +13,9 @@
 CHIPS = 64
 FIELDS, LEVELS, LANES = 5, 128, 128
 BLOCKS, STEPS = 8, 16
-ROWS = 10
-ROOT = 13
+ROWS = 9
+ROOT = 12
+ORDER = range(1, CHIPS)
 F32, BF16 = jnp.float32, jnp.bfloat16
 
 
@@ -34,7 +35,8 @@
 def kernel(
     x_hbm, k_hbm, flux_hbm, assign_hbm, out,
     xin, target, small, buf, recv, halo, packed, base, work, edge_out, edge_in, hot, kappa_t,
-    local_sem, swap_send, swap_recv, halo_send, halo_recv, edge_send, edge_recv, all_send, all_recv, go_sem,
+    local_sem, swap_send, swap_recv, halo_send, halo_recv, edge_send, edge_recv, all_send, all_recv,
+    go_sem, up_sem, down_sem,
 ):
     f, c = lax.axis_index("face"), lax.axis_index("col")
     y, core = c >> 1, c & 1
@@ -43,13 +45,21 @@
     partner = (f, c ^ 1)
     is_root = f == ROOT
 
+    z = f & 3
     barrier = pltpu.get_barrier_semaphore()
     for r in range(COLS):
         @pl.when(jnp.logical_not(is_root & (c == r)))
         def _():
             pl.semaphore_signal(barrier, inc=1, device_id=(ROOT, r), device_id_type=MESH)
-    for peer in ((up, c), (down, c), partner):
-        pl.semaphore_signal(barrier, inc=1, device_id=peer, device_id_type=MESH)
+    pl.semaphore_signal(barrier, inc=1, device_id=partner, device_id_type=MESH)
+
+    @pl.when(z != 3)
+    def _():
+        pl.semaphore_signal(barrier, inc=1, device_id=(up, c), device_id_type=MESH)
+
+    @pl.when(z == 0)
+    def _():
+        pl.semaphore_signal(barrier, inc=1, device_id=(down, c), device_id_type=MESH)
 
     local = [
         pltpu.make_async_copy(x_hbm, xin, local_sem.at[0]),
@@ -59,16 +69,6 @@
     ]
     for copy in local:
         copy.start()
-
-    @pl.when(is_root)
-    def _():
-        pl.semaphore_wait(barrier, 3 + FACES * COLS - 1)
-        for i in [j for j in range(FACES) if j != ROOT]:
-            pl.semaphore_signal(go_sem, inc=1, device_id=(i, c), device_id_type=MESH)
-
-    @pl.when(jnp.logical_not(is_root))
-    def _():
-        pl.semaphore_wait(barrier, 3)
 
     swaps = [
         pltpu.make_async_remote_copy(
@@ -80,20 +80,65 @@
             (flux_hbm, small.at[core]),
         ))
     ]
-    for copy in swaps:
-        copy.start()
-
-    halos = []
-    for fl in range(FIELDS):
-        at = pl.ds(fl * LEVELS, LEVELS)
-        for d, row, peer in ((0, 1, up), (1, 0, down)):
-            copy = pltpu.make_async_remote_copy(
-                src_ref=x_hbm.at[at, row], dst_ref=halo.at[d, at],
+    halos = [
+        [
+            pltpu.make_async_remote_copy(
+                src_ref=x_hbm.at[pl.ds(fl * LEVELS, LEVELS), row], dst_ref=halo.at[d, pl.ds(fl * LEVELS, LEVELS)],
                 send_sem=halo_send.at[d, fl], recv_sem=halo_recv.at[d, fl],
                 device_id=(peer, c), device_id_type=MESH,
             )
-            copy.start()
-            halos.append(copy)
+            for fl in range(FIELDS)
+        ]
+        for d, row, peer in ((0, 1, up), (1, 0, down))
+    ]
+
+    @pl.when(jnp.logical_not(is_root))
+    def _():
+        @pl.when((z == 1) | (z == 2))
+        def _():
+            pl.semaphore_wait(barrier, 2)
+
+        @pl.when(z == 3)
+        def _():
+            pl.semaphore_wait(barrier, 3)
+
+        @pl.when(z == 0)
+        def _():
+            pl.semaphore_wait(barrier, 1)
+
+        for copy in swaps:
+            copy.start()
+
+    @pl.when(z == 3)
+    def _():
+        pl.semaphore_signal(down_sem, inc=1, device_id=(up, c), device_id_type=MESH)
+
+    @pl.when(z != 0)
+    def _():
+        pl.semaphore_signal(up_sem, inc=1, device_id=(down, c), device_id_type=MESH)
+        for copy in halos[1][:3]:
+            copy.start()
+
+    @pl.when(z != 3)
+    def _():
+        pl.semaphore_wait(up_sem, 1)
+
+    for copy in halos[0][:3]:
+        copy.start()
+
+    @pl.when(z == 0)
+    def _():
+        pl.semaphore_wait(down_sem, 1)
+        for copy in halos[1][:3]:
+            copy.start()
+
+    @pl.when(is_root)
+    def _():
+        pl.semaphore_wait(barrier, FACES * COLS)
+        for i in [n for n in range(FACES) if n != ROOT]:
+            pl.semaphore_signal(go_sem, inc=1, device_id=(i, c), device_id_type=MESH)
+        for copy in swaps:
+            copy.start()
 
     lane = lax.broadcasted_iota(jnp.int32, (8, LANES), 1)
     sub = lax.broadcasted_iota(jnp.int32, (8, LANES), 0)
@@ -119,20 +164,29 @@
     local[3].wait()
     for copy in swaps:
         copy.wait_recv()
-    for s in range(2):
-        for g in range(4):
-            buf[pl.ds(16 * g, 16), 8 + s] = jnp.broadcast_to(small[s, g], (16, 1, LANES))
+    high = (lax.broadcasted_iota(jnp.int32, (1, LANES), 1) & 4) != 0
+    for g in range(4):
+        first, second = small[0, g], small[1, g]
+        both = jnp.where(
+            core == 0,
+            jnp.where(high, pltpu.roll(second, 4, axis=1), first),
+            jnp.where(high, second, pltpu.roll(first, LANES - 4, axis=1)),
+        )
+        buf[pl.ds(16 * g, 16), 8] = jnp.broadcast_to(both, (16, 1, LANES))
 
     @pl.when(jnp.logical_not(is_root))
     def _():
         pl.semaphore_wait(go_sem, 1)
 
-    for i in range(1, CHIPS):
+    for i in ORDER:
         pf, py = (f + (i >> 2)) & 15, (y + (i & 3)) & 3
         pltpu.make_async_remote_copy(
             src_ref=buf.at[pf * 4 + py], dst_ref=recv.at[chip], send_sem=all_send, recv_sem=all_recv,
             device_id=(pf, py * 2 + core), device_id_type=MESH,
         ).start()
+    for pair in zip(halos[0][3:], halos[1][3:]):
+        for copy in pair:
+            copy.start()
     own = pltpu.make_async_copy(buf.at[chip], recv.at[chip], local_sem.at[4])
     own.start()
     edge_copies = [
@@ -182,14 +236,9 @@
     columns = lookup(received[...], hot[...])
     kappa_t[0] = columns[:, :LANES]
     kappa_t[1] = columns[:, LANES:]
-    flux_rows = jnp.concatenate(
-        [received[pl.ds(8, CHIPS, stride=ROWS), :], received[pl.ds(9, CHIPS, stride=ROWS), :]], axis=0
-    )
-    flux_hot = (
-        lax.broadcasted_iota(jnp.int32, (FACES * COLS, 256), 0) == (t >> 1) + (t & 1) * CHIPS
-    ).astype(F32)
-    flux = lookup(flux_rows, flux_hot.astype(BF16))
-    wanted = rank + ((f & 3) * 32 + c * 4).astype(F32)
+    flux_hot = (lax.broadcasted_iota(jnp.int32, (CHIPS, 256), 0) == (t >> 1)).astype(F32)
+    flux = lookup(received[pl.ds(8, CHIPS, stride=ROWS), :], flux_hot.astype(BF16))
+    wanted = rank + ((t & 1) * 4 + ((f & 3) * 32 + y * 8)).astype(F32)
     lanes_at = lax.broadcasted_iota(jnp.int32, (LANES, 256), 0).astype(F32)
     heat = jnp.sum(jnp.where(lanes_at == wanted, flux, 0.0), axis=0, keepdims=True)
     heat = [jnp.where(sub == BLOCKS - 1, heat[:, r * LANES : (r + 1) * LANES], 0.0) for r in range(2)]
@@ -258,10 +307,9 @@
 
     halo_rows = halo.reshape(2 * FIELDS * LEVELS, LANES)
     out_rows = out.reshape(FIELDS * LEVELS * 2, LANES)
-    outs = []
     for fl in range(FIELDS):
         for d_at in range(2):
-            halos[2 * fl + d_at].wait_recv()
+            halos[d_at][fl].wait_recv()
         for j in range(STEPS):
             for r in range(2):
                 beside = halo_rows[pl.ds((r * FIELDS + fl) * LEVELS + j, BLOCKS, stride=STEPS), :]
@@ -269,10 +317,8 @@
                     base[r, fl, j] + SMOOTHING * beside
                 )
     pltpu.make_async_copy(recv.at[pl.ds(0, CHIPS - 1)], recv.at[pl.ds(0, CHIPS - 1)], all_send).wait()
-    for copy in swaps + edge_copies + halos:
+    for copy in swaps + edge_copies + halos[0] + halos[1]:
         copy.wait_send()
-    for copy in outs:
-        copy.wait()
 
 
 def shards(prognostic, diffusivity, surface_flux, assignment):
@@ -313,6 +359,8 @@
             dma,
             dma,
             pltpu.SemaphoreType.REGULAR,
+            pltpu.SemaphoreType.REGULAR,
+            pltpu.SemaphoreType.REGULAR,
         ],
         compiler_params=pltpu.CompilerParams(
             collective_id=0, has_side_effects=True, vmem_limit_bytes=56 << 20

time: 23.9 us -> 21.5 us (0.90)
  Pallas kernels: 22.7 us -> 20.5 us
    pallas_call x1, Pallas kernels: 22.7 us -> 20.5 us  [shards(): pl.pallas_call(kernel, out_shape=pltpu.VMEM(x.shape, F32), name='exchange...]
where the time goes in v2:
time: 21.5 us; the launch traced here: 21.3 us
  Pallas kernels  20.5 us (95%)
  local copies, waits for them, and re-layouts  0.84 us (4%)
    pallas_call x1, Pallas kernels, shards(): pl.pallas_call(kernel, out_shape=pltpu.VMEM(x.shape, F32), name='exchange...  20.5 us
    unnamed x1, local copies, waits for them, and re-layouts  0.84 us

profile of v2, /device:TPU:1, one launch (start us, length us, event | category | flops | bytes accessed | tf_op | source)
XLA Modules:
  0.0 21.3 jit_solution(7669221568137670588)
XLA Ops:
  0.0 20.5 %exchange.1 = f32[640,2,1,128]{3,2,1,0:T(1,128)S(1)} custom-call(f32[640,2,1,128]{3,2,1,0:T(1,128)} %bitcast.6, f32[64,2,4,1,128]{4,3,2,1,0:T(1,128)} %bitcast.7, f32[4,1,128]{2,1,0:T(1,128)} %bitcast.8, s32[1,256]{1,0:T(1,128)} %bitcast.9), custom_call_target="tpu_custom_call" | custom-call | tf_op jit(solution)/shard_map/exchange/pallas_call | solution.py:332
  20.5 0.8 %copy.6 = f32[5,128,2,128]{3,2,1,0:T(2,128)} copy(f32[5,128,2,128]{3,2,1,0:T(2,128)S(1)} %bitcast.5) | data formatting | bytes 1310720

commit v3 on v2

--- a/solution.py
+++ b/solution.py
@@ -14,8 +14,7 @@
 FIELDS, LEVELS, LANES = 5, 128, 128
 BLOCKS, STEPS = 8, 16
 ROWS = 9
-ROOT = 12
-ORDER = range(1, CHIPS)
+AHEAD = 2
 F32, BF16 = jnp.float32, jnp.bfloat16
 
 
@@ -36,30 +35,21 @@
     x_hbm, k_hbm, flux_hbm, assign_hbm, out,
     xin, target, small, buf, recv, halo, packed, base, work, edge_out, edge_in, hot, kappa_t,
     local_sem, swap_send, swap_recv, halo_send, halo_recv, edge_send, edge_recv, all_send, all_recv,
-    go_sem, up_sem, down_sem,
+    go_sem, near_sem,
 ):
     f, c = lax.axis_index("face"), lax.axis_index("col")
     y, core = c >> 1, c & 1
     chip = f * 4 + y
     up, down = (f + 1) & 15, (f + 15) & 15
     partner = (f, c ^ 1)
-    is_root = f == ROOT
-
-    z = f & 3
+
     barrier = pltpu.get_barrier_semaphore()
-    for r in range(COLS):
-        @pl.when(jnp.logical_not(is_root & (c == r)))
-        def _():
-            pl.semaphore_signal(barrier, inc=1, device_id=(ROOT, r), device_id_type=MESH)
-    pl.semaphore_signal(barrier, inc=1, device_id=partner, device_id_type=MESH)
-
-    @pl.when(z != 3)
-    def _():
-        pl.semaphore_signal(barrier, inc=1, device_id=(up, c), device_id_type=MESH)
-
-    @pl.when(z == 0)
-    def _():
-        pl.semaphore_signal(barrier, inc=1, device_id=(down, c), device_id_type=MESH)
+    first, second = y << 1, (y << 1) | 1
+    for i in range(1, FACES):
+        pl.semaphore_signal(barrier, inc=1, device_id=((f + i) & 15, second), device_id_type=MESH)
+    y_peers = [(f, (((y + i) & 3) << 1) | 1) for i in range(1, 4)]
+    for peer in y_peers + [(up, first), (down, first), partner]:
+        pl.semaphore_signal(barrier, inc=1, device_id=peer, device_id_type=MESH)
 
     local = [
         pltpu.make_async_copy(x_hbm, xin, local_sem.at[0]),
@@ -92,53 +82,26 @@
         for d, row, peer in ((0, 1, up), (1, 0, down))
     ]
 
-    @pl.when(jnp.logical_not(is_root))
-    def _():
-        @pl.when((z == 1) | (z == 2))
-        def _():
-            pl.semaphore_wait(barrier, 2)
-
-        @pl.when(z == 3)
-        def _():
-            pl.semaphore_wait(barrier, 3)
-
-        @pl.when(z == 0)
-        def _():
-            pl.semaphore_wait(barrier, 1)
-
-        for copy in swaps:
+    @pl.when(core == 0)
+    def _():
+        pl.semaphore_wait(barrier, 5)
+        pl.semaphore_signal(near_sem, inc=1, device_id=partner, device_id_type=MESH)
+
+    @pl.when(core == 1)
+    def _():
+        pl.semaphore_wait(near_sem, 1)
+
+    for pair in zip(halos[0][:AHEAD], halos[1][:AHEAD]):
+        for copy in pair:
             copy.start()
-
-    @pl.when(z == 3)
-    def _():
-        pl.semaphore_signal(down_sem, inc=1, device_id=(up, c), device_id_type=MESH)
-
-    @pl.when(z != 0)
-    def _():
-        pl.semaphore_signal(up_sem, inc=1, device_id=(down, c), device_id_type=MESH)
-        for copy in halos[1][:3]:
-            copy.start()
-
-    @pl.when(z != 3)
-    def _():
-        pl.semaphore_wait(up_sem, 1)
-
-    for copy in halos[0][:3]:
+    for copy in swaps:
         copy.start()
 
-    @pl.when(z == 0)
-    def _():
-        pl.semaphore_wait(down_sem, 1)
-        for copy in halos[1][:3]:
-            copy.start()
-
-    @pl.when(is_root)
-    def _():
-        pl.semaphore_wait(barrier, FACES * COLS)
-        for i in [n for n in range(FACES) if n != ROOT]:
-            pl.semaphore_signal(go_sem, inc=1, device_id=(i, c), device_id_type=MESH)
-        for copy in swaps:
-            copy.start()
+    @pl.when(core == 1)
+    def _():
+        pl.semaphore_wait(barrier, 2 * (FACES - 1 + 3) + 1)
+        for peer in y_peers:
+            pl.semaphore_signal(go_sem, inc=1, device_id=peer, device_id_type=MESH)
 
     lane = lax.broadcasted_iota(jnp.int32, (8, LANES), 1)
     sub = lax.broadcasted_iota(jnp.int32, (8, LANES), 0)
@@ -174,17 +137,24 @@
         )
         buf[pl.ds(16 * g, 16), 8] = jnp.broadcast_to(both, (16, 1, LANES))
 
-    @pl.when(jnp.logical_not(is_root))
-    def _():
-        pl.semaphore_wait(go_sem, 1)
-
-    for i in ORDER:
-        pf, py = (f + (i >> 2)) & 15, (y + (i & 3)) & 3
+    def send(pf, py):
         pltpu.make_async_remote_copy(
             src_ref=buf.at[pf * 4 + py], dst_ref=recv.at[chip], send_sem=all_send, recv_sem=all_recv,
             device_id=(pf, py * 2 + core), device_id_type=MESH,
         ).start()
-    for pair in zip(halos[0][3:], halos[1][3:]):
+
+    @pl.when(core == 1)
+    def _():
+        pl.semaphore_wait(go_sem, len(y_peers))
+        pl.semaphore_signal(near_sem, inc=1, device_id=partner, device_id_type=MESH)
+
+    @pl.when(core == 0)
+    def _():
+        pl.semaphore_wait(near_sem, 1)
+
+    for i in range(1, CHIPS):
+        send((f + (i >> 2)) & 15, (y + (i & 3)) & 3)
+    for pair in zip(halos[0][AHEAD:], halos[1][AHEAD:]):
         for copy in pair:
             copy.start()
     own = pltpu.make_async_copy(buf.at[chip], recv.at[chip], local_sem.at[4])
@@ -360,7 +330,6 @@
             dma,
             pltpu.SemaphoreType.REGULAR,
             pltpu.SemaphoreType.REGULAR,
-            pltpu.SemaphoreType.REGULAR,
         ],
         compiler_params=pltpu.CompilerParams(
             collective_id=0, has_side_effects=True, vmem_limit_bytes=56 << 20

time: 21.5 us -> 21.3 us (level)
  no operation moved by 1% of the time
where the time goes in v3:
time: 21.3 us; the launch traced here: 21.2 us
  Pallas kernels  20.3 us (95%)
  local copies, waits for them, and re-layouts  0.84 us (4%)
    pallas_call x1, Pallas kernels, shards(): pl.pallas_call(kernel, out_shape=pltpu.VMEM(x.shape, F32), name='exchange...  20.3 us
    unnamed x1, local copies, waits for them, and re-layouts  0.84 us

profile of v3, /device:TPU:1, one launch (start us, length us, event | category | flops | bytes accessed | tf_op | source)
XLA Modules:
  0.0 21.2 jit_solution(16691601780068235203)
XLA Ops:
  0.0 20.3 %exchange.1 = f32[640,2,1,128]{3,2,1,0:T(1,128)S(1)} custom-call(f32[640,2,1,128]{3,2,1,0:T(1,128)} %bitcast.6, f32[64,2,4,1,128]{4,3,2,1,0:T(1,128)} %bitcast.7, f32[4,1,128]{2,1,0:T(1,128)} %bitcast.8, s32[1,256]{1,0:T(1,128)} %bitcast.9), custom_call_target="tpu_custom_call" | custom-call | tf_op jit(solution)/shard_map/exchange/pallas_call | solution.py:302
  20.3 0.8 %copy.6 = f32[5,128,2,128]{3,2,1,0:T(2,128)} copy(f32[5,128,2,128]{3,2,1,0:T(2,128)S(1)} %bitcast.5) | data formatting | bytes 1310720

commit v4 on v3

--- a/solution.py
+++ b/solution.py
@@ -97,6 +97,11 @@
     for copy in swaps:
         copy.start()
 
+    @pl.when(y < 2)
+    def _():
+        for n in range(2):
+            halos[n][2].start()
+
     @pl.when(core == 1)
     def _():
         pl.semaphore_wait(barrier, 2 * (FACES - 1 + 3) + 1)
@@ -154,7 +159,13 @@
 
     for i in range(1, CHIPS):
         send((f + (i >> 2)) & 15, (y + (i & 3)) & 3)
-    for pair in zip(halos[0][AHEAD:], halos[1][AHEAD:]):
+
+    @pl.when(jnp.logical_not(y < 2))
+    def _():
+        for n in range(2):
+            halos[n][2].start()
+
+    for pair in zip(halos[0][AHEAD + 1:], halos[1][AHEAD + 1:]):
         for copy in pair:
             copy.start()
     own = pltpu.make_async_copy(buf.at[chip], recv.at[chip], local_sem.at[4])

time: 21.3 us -> 20.8 us (0.977)
  Pallas kernels: 20.3 us -> 19.9 us
    pallas_call x1, Pallas kernels: 20.3 us -> 19.9 us  [shards(): pl.pallas_call(kernel, out_shape=pltpu.VMEM(x.shape, F32), name='exchange...]
where the time goes in v4:
time: 20.8 us; the launch traced here: 20.7 us
  Pallas kernels  19.9 us (96%)
  local copies, waits for them, and re-layouts  0.84 us (4%)
    pallas_call x1, Pallas kernels, shards(): pl.pallas_call(kernel, out_shape=pltpu.VMEM(x.shape, F32), name='exchange...  19.9 us
    unnamed x1, local copies, waits for them, and re-layouts  0.84 us

profile of v4, /device:TPU:1, one launch (start us, length us, event | category | flops | bytes accessed | tf_op | source)
XLA Modules:
  0.0 20.7 jit_solution(2571567485258992317)
XLA Ops:
  0.0 19.9 %exchange.1 = f32[640,2,1,128]{3,2,1,0:T(1,128)S(1)} custom-call(f32[640,2,1,128]{3,2,1,0:T(1,128)} %bitcast.6, f32[64,2,4,1,128]{4,3,2,1,0:T(1,128)} %bitcast.7, f32[4,1,128]{2,1,0:T(1,128)} %bitcast.8, s32[1,256]{1,0:T(1,128)} %bitcast.9), custom_call_target="tpu_custom_call" | custom-call | tf_op jit(solution)/shard_map/exchange/pallas_call | solution.py:313
  19.9 0.8 %copy.6 = f32[5,128,2,128]{3,2,1,0:T(2,128)} copy(f32[5,128,2,128]{3,2,1,0:T(2,128)S(1)} %bitcast.5) | data formatting | bytes 1310720

commit v5 on v4

--- a/solution.py
+++ b/solution.py
@@ -105,7 +105,7 @@
     @pl.when(core == 1)
     def _():
         pl.semaphore_wait(barrier, 2 * (FACES - 1 + 3) + 1)
-        for peer in y_peers:
+        for peer in y_peers + [(pf, pc ^ 1) for pf, pc in y_peers] + [partner]:
             pl.semaphore_signal(go_sem, inc=1, device_id=peer, device_id_type=MESH)
 
     lane = lax.broadcasted_iota(jnp.int32, (8, LANES), 1)
@@ -151,11 +151,10 @@
     @pl.when(core == 1)
     def _():
         pl.semaphore_wait(go_sem, len(y_peers))
-        pl.semaphore_signal(near_sem, inc=1, device_id=partner, device_id_type=MESH)
 
     @pl.when(core == 0)
     def _():
-        pl.semaphore_wait(near_sem, 1)
+        pl.semaphore_wait(go_sem, len(y_peers) + 1)
 
     for i in range(1, CHIPS):
         send((f + (i >> 2)) & 15, (y + (i & 3)) & 3)

time: 20.8 us -> 20.8 us (level)
  no operation moved by 1% of the time
where the time goes in v5:
time: 20.8 us; the launch traced here: 20.7 us
  Pallas kernels  19.9 us (96%)
  local copies, waits for them, and re-layouts  0.84 us (4%)
    pallas_call x1, Pallas kernels, shards(): pl.pallas_call(kernel, out_shape=pltpu.VMEM(x.shape, F32), name='exchange...  19.9 us
    unnamed x1, local copies, waits for them, and re-layouts  0.84 us

profile of v5, /device:TPU:1, one launch (start us, length us, event | category | flops | bytes accessed | tf_op | source)
XLA Modules:
  0.0 20.7 jit_solution(16739822775619118104)
XLA Ops:
  0.0 19.9 %exchange.1 = f32[640,2,1,128]{3,2,1,0:T(1,128)S(1)} custom-call(f32[640,2,1,128]{3,2,1,0:T(1,128)} %bitcast.6, f32[64,2,4,1,128]{4,3,2,1,0:T(1,128)} %bitcast.7, f32[4,1,128]{2,1,0:T(1,128)} %bitcast.8, s32[1,256]{1,0:T(1,128)} %bitcast.9), custom_call_target="tpu_custom_call" | custom-call | tf_op jit(solution)/shard_map/exchange/pallas_call | solution.py:312
  19.9 0.8 %copy.6 = f32[5,128,2,128]{3,2,1,0:T(2,128)} copy(f32[5,128,2,128]{3,2,1,0:T(2,128)S(1)} %bitcast.5) | data formatting | bytes 1310720
